TPU v7x, 256 devices: a whole 4x4x8 slice. The times are simulated.
256 devices in a mesh: shard: 8 (over z_hi, core), replica: 32 (over x, z_lo, y).
Axes of the slice: x: 4, y: 4, z: 8 (z_hi: 4, z_lo: 2; z = z_hi * 2 + z_lo), core: 2. Of those that a mesh axis runs over, the one named last changes fastest.
Arguments:
- tokens: bfloat16 [40960, 1024], P(('shard', 'replica')), may hold values from -6 to 6
- cotangent: bfloat16 [40960, 1024], P(('shard', 'replica')), may hold values from -6 to 6
- gain_one: bfloat16 [1024], P('shard'), may hold values from 0.5 to 1.5
- gain_two: bfloat16 [1024], P('shard'), may hold values from 0.5 to 1.5
- w_qkv: bfloat16 [1024, 2048], P('shard'), may hold values from -0.1875 to 0.1875
- w_out: bfloat16 [1024, 1024], P(None, 'shard'), may hold values from -1.5 to 1.5
- w_router: bfloat16 [1024, 10], P('shard'), may hold values from -0.09375 to 0.09375
- w_gate_up: bfloat16 [10, 1024, 1024], P(None, 'shard'), may hold values from -0.1875 to 0.1875
- w_down: bfloat16 [10, 512, 1024], P(None, None, 'shard'), may hold values from -1 to 1
- routes: int32 [40960, 8], P(('shard', 'replica')), may hold values from 0 to 9, all different within a row
- slot_order: int32 [256, 1280], P(('shard', 'replica')), may hold values from 0 to 1279, each once within a row
Outputs:
- layer_out: bfloat16 [40960, 1024], P(('shard', 'replica'))
- grad_tokens: bfloat16 [40960, 1024], P(('shard', 'replica'))
- grad_gain_one: float32 [1024], P('shard')
- grad_gain_two: float32 [1024], P('shard')
- grad_qkv: float32 [1024, 2048], P('shard')
- grad_out: float32 [1024, 1024], P(None, 'shard')
- grad_router: float32 [1024, 10], P('shard')
- grad_gate_up: float32 [10, 1024, 1024], P(None, 'shard')
- grad_down: float32 [10, 512, 1024], P(None, None, 'shard')
Inputs may be any that keep to these rules, and one draw needn't show every extreme that they name: `routes`: each row names 8 different experts. `slot_order`: each row is a permutation of one device's pairs t * 8 + r.
All inputs are finite; a program needn't handle non-finite values.
Results may differ from a plain program's by a relative error of at most 0.03.
Values may be sent and summed in bfloat16 or wider, within the bound.
No kernel may reach another device: no remote copies, remote signals or barrier semaphores. Data moves between devices by JAX's collectives and lax.ppermute only.
A program may use at most 192 MiB of HBM per device.

v0:
```python
import math

import jax
import jax.numpy as jnp
from jax import lax
from jax.sharding import PartitionSpec as P

D = 1024
HEADS = 16
KV_HEADS = 8
HD = 64
F = 512
TOPK = 8
EXPERTS = 10
CAP = 144


EPSILON = 1e-06
ROPE_BASE = 10000.0


def rope_tables(length, head_size):
    half_width = head_size // 2
    position = jnp.arange(length).astype(jnp.float32)[:, None]
    frequency = ROPE_BASE ** (-jnp.arange(half_width).astype(jnp.float32) / half_width)
    angles = position * frequency[None, :]
    return (jnp.cos(angles)[:, None, :], jnp.sin(angles)[:, None, :])


def rotate(values, cosine, sine, direction):
    half_width = values.shape[-1] // 2
    first = values[..., :half_width]
    second = values[..., half_width:]
    return jnp.concatenate(
        [first * cosine - direction * second * sine, second * cosine + direction * first * sine],
        axis=-1,
    )


def slot_plan(route_ids, order_row):
    pair_expert = route_ids.reshape(-1)
    ordered = pair_expert[order_row]
    onehot_rows = (ordered[:, None] == jnp.arange(EXPERTS, dtype=jnp.int32)[None, :]).astype(
        jnp.int32
    )
    earlier = jnp.cumsum(onehot_rows, axis=0) - onehot_rows
    ordered_slot = jnp.sum(earlier * onehot_rows, axis=1)
    pair_slot = jnp.zeros_like(pair_expert).at[order_row].set(ordered_slot)
    total_slots = EXPERTS * CAP
    target = jnp.where(pair_slot < CAP, pair_expert * CAP + pair_slot, total_slots)
    pair_count = pair_expert.shape[0]
    pair_table = (
        jnp.full((total_slots + 1,), pair_count, jnp.int32)
        .at[target]
        .set(jnp.arange(pair_count, dtype=jnp.int32))
    )
    return (target, pair_table[:total_slots])


def shards(
    tokens,
    cotangent,
    gain_one,
    gain_two,
    w_qkv,
    w_out,
    w_router,
    w_gate_up,
    w_down,
    routes,
    slot_order,
):
    shard_parts = (gain_one, gain_two, w_qkv, w_out, w_router, w_gate_up, w_down)
    gathered = (
        lax.all_gather(shard_parts[0], "shard", axis=0, tiled=True),
        lax.all_gather(shard_parts[1], "shard", axis=0, tiled=True),
        lax.all_gather(shard_parts[2], "shard", axis=0, tiled=True),
        lax.all_gather(shard_parts[3], "shard", axis=1, tiled=True),
        lax.all_gather(shard_parts[4], "shard", axis=0, tiled=True),
        lax.all_gather(shard_parts[5], "shard", axis=1, tiled=True),
        lax.all_gather(shard_parts[6], "shard", axis=2, tiled=True),
    )
    gain_a, gain_b, qkv_full, out_full, router_full, gate_up_full, down_full = gathered
    length = tokens.shape[0]
    width_q = HEADS * HD
    width_k = KV_HEADS * HD
    group_size = HEADS // KV_HEADS
    scale = 1.0 / math.sqrt(HD)
    target, pair_table = slot_plan(routes, slot_order[0])
    cosine, sine = rope_tables(length, HD)
    causal = jnp.arange(length)[:, None] >= jnp.arange(length)[None, :]
    hidden_in = tokens.astype(jnp.float32)
    rstd_one = lax.rsqrt(jnp.mean(hidden_in * hidden_in, axis=-1, keepdims=True) + EPSILON)
    norm_one = hidden_in * rstd_one
    gain_af = gain_a.astype(jnp.float32)
    normed = (norm_one * gain_af).astype(jnp.bfloat16)
    projected = jnp.dot(normed, qkv_full, preferred_element_type=jnp.float32)
    queries = rotate(projected[:, :width_q].reshape(length, HEADS, HD), cosine, sine, 1.0).astype(
        jnp.bfloat16
    )
    key_rows = rotate(
        projected[:, width_q : width_q + width_k].reshape(length, KV_HEADS, HD), cosine, sine, 1.0
    ).astype(jnp.bfloat16)
    value_rows = (
        projected[:, width_q + width_k :].reshape(length, KV_HEADS, HD).astype(jnp.bfloat16)
    )
    grouped = queries.reshape(length, KV_HEADS, group_size, HD)
    scores = (
        jnp.einsum("qhgd,khd->hgqk", grouped, key_rows, preferred_element_type=jnp.float32) * scale
    )
    scores = jnp.where(causal, scores, -1e30)
    row_max = jnp.max(scores, axis=-1, keepdims=True)
    shifted = jnp.exp(scores - row_max)
    row_total = jnp.sum(shifted, axis=-1, keepdims=True)
    log_total = row_max + jnp.log(row_total)
    probs = (shifted / row_total).astype(jnp.bfloat16)
    attended = jnp.einsum("hgqk,khd->qhgd", probs, value_rows, preferred_element_type=jnp.float32)
    attended = attended.reshape(length, width_q).astype(jnp.bfloat16)
    middle = hidden_in + jnp.dot(attended, out_full, preferred_element_type=jnp.float32)
    rstd_two = lax.rsqrt(jnp.mean(middle * middle, axis=-1, keepdims=True) + EPSILON)
    norm_two = middle * rstd_two
    gain_bf = gain_b.astype(jnp.float32)
    normed_two = (norm_two * gain_bf).astype(jnp.bfloat16)
    logits = jnp.dot(normed_two, router_full, preferred_element_type=jnp.float32)
    chosen = jnp.take_along_axis(logits, routes, axis=1)
    gates = jax.nn.softmax(chosen, axis=-1)
    padded = jnp.concatenate([normed_two, jnp.zeros((1, D), jnp.bfloat16)], axis=0)
    slot_rows = padded[pair_table // TOPK].reshape(EXPERTS, CAP, D)
    gate_up = jnp.einsum(
        "ecd,edf->ecf", slot_rows, gate_up_full, preferred_element_type=jnp.float32
    )
    gate_part = gate_up[..., :F]
    up_part = gate_up[..., F:]
    sigmoid_gate = jax.nn.sigmoid(gate_part)
    silu_gate = gate_part * sigmoid_gate
    activated = (silu_gate * up_part).astype(jnp.bfloat16)
    expert_out = jnp.einsum(
        "ecf,efd->ecd", activated, down_full, preferred_element_type=jnp.float32
    ).reshape(EXPERTS * CAP, D)
    expert_pad = jnp.concatenate([expert_out, jnp.zeros((1, D), jnp.float32)], axis=0)
    returned = expert_pad[target].reshape(length, TOPK, D)
    mixture = jnp.sum(gates[:, :, None] * returned, axis=1)
    layer_out = (middle + mixture).astype(jnp.bfloat16)
    unused_a, unused_b, qkv_back, out_back, router_back, gate_up_back, down_back = gathered
    upstream = cotangent.astype(jnp.float32)
    gate_flat = jnp.concatenate([gates.reshape(-1), jnp.zeros((1,), jnp.float32)], axis=0)
    up_pad = jnp.concatenate([upstream, jnp.zeros((1, D), jnp.float32)], axis=0)
    slot_grad = (
        (gate_flat[pair_table][:, None] * up_pad[pair_table // TOPK])
        .astype(jnp.bfloat16)
        .reshape(EXPERTS, CAP, D)
    )
    gate_grad = jnp.einsum("td,tkd->tk", upstream, returned)
    grad_down = jnp.einsum("ecf,ecd->efd", activated, slot_grad, preferred_element_type=jnp.float32)
    act_grad = jnp.einsum("ecd,efd->ecf", slot_grad, down_back, preferred_element_type=jnp.float32)
    gate_deriv = act_grad * up_part * sigmoid_gate * (1.0 + gate_part * (1.0 - sigmoid_gate))
    up_deriv = act_grad * silu_gate
    gate_up_grad = jnp.concatenate([gate_deriv, up_deriv], axis=-1).astype(jnp.bfloat16)
    grad_gate_up = jnp.einsum(
        "ecd,ecf->edf", slot_rows, gate_up_grad, preferred_element_type=jnp.float32
    )
    slot_in_grad = jnp.einsum(
        "ecf,edf->ecd", gate_up_grad, gate_up_back, preferred_element_type=jnp.float32
    )
    slot_pad = jnp.concatenate(
        [slot_in_grad.reshape(EXPERTS * CAP, D), jnp.zeros((1, D), jnp.float32)], axis=0
    )
    norm_two_grad = jnp.sum(slot_pad[target].reshape(length, TOPK, D), axis=1)
    chosen_grad = gates * (gate_grad - jnp.sum(gates * gate_grad, axis=1, keepdims=True))
    expert_match = (
        routes[:, :, None] == jnp.arange(EXPERTS, dtype=jnp.int32)[None, None, :]
    ).astype(jnp.float32)
    logit_grad = jnp.sum(expert_match * chosen_grad[:, :, None], axis=1).astype(jnp.bfloat16)
    grad_router = jnp.dot(normed_two.T, logit_grad, preferred_element_type=jnp.float32)
    norm_two_grad = norm_two_grad + jnp.dot(
        logit_grad, router_back.T, preferred_element_type=jnp.float32
    )
    grad_gain_two = jnp.sum(norm_two_grad * norm_two, axis=0)
    scaled_two = norm_two_grad * gain_bf
    middle_grad = upstream + rstd_two * (
        scaled_two - norm_two * jnp.mean(scaled_two * norm_two, axis=-1, keepdims=True)
    )
    middle_low = middle_grad.astype(jnp.bfloat16)
    grad_out = jnp.dot(attended.T, middle_low, preferred_element_type=jnp.float32)
    attended_grad = jnp.dot(middle_low, out_back.T, preferred_element_type=jnp.float32)
    attended_grad = attended_grad.astype(jnp.bfloat16).reshape(length, KV_HEADS, group_size, HD)

    def head_backward(pieces):
        query_head, key_head, value_head, out_grad_head, total_head = pieces
        head_scores = (
            jnp.einsum("qgd,kd->gqk", query_head, key_head, preferred_element_type=jnp.float32)
            * scale
        )
        head_scores = jnp.where(causal[None, :, :], head_scores, -1e30)
        head_probs = jnp.exp(head_scores - total_head)
        head_low = head_probs.astype(jnp.bfloat16)
        head_pgrad = jnp.einsum(
            "qgd,kd->gqk", out_grad_head, value_head, preferred_element_type=jnp.float32
        )
        head_vgrad = jnp.einsum(
            "gqk,qgd->kd", head_low, out_grad_head, preferred_element_type=jnp.float32
        )
        head_sgrad = head_probs * (
            head_pgrad - jnp.sum(head_probs * head_pgrad, axis=-1, keepdims=True)
        )
        head_sgrad = head_sgrad.astype(jnp.bfloat16)
        head_qgrad = (
            jnp.einsum("gqk,kd->qgd", head_sgrad, key_head, preferred_element_type=jnp.float32)
            * scale
        )
        head_kgrad = (
            jnp.einsum("gqk,qgd->kd", head_sgrad, query_head, preferred_element_type=jnp.float32)
            * scale
        )
        return (head_qgrad, head_kgrad, head_vgrad)

    per_head = (
        grouped.transpose(1, 0, 2, 3),
        key_rows.transpose(1, 0, 2),
        value_rows.transpose(1, 0, 2),
        attended_grad.transpose(1, 0, 2, 3),
        log_total,
    )
    query_heads, key_heads, value_heads = lax.map(head_backward, per_head)
    query_grad = query_heads.transpose(1, 0, 2, 3).reshape(length, HEADS, HD)
    key_grad = key_heads.transpose(1, 0, 2)
    value_grad = value_heads.transpose(1, 0, 2)
    query_grad = rotate(query_grad, cosine, sine, -1.0).reshape(length, width_q)
    key_grad = rotate(key_grad, cosine, sine, -1.0).reshape(length, width_k)
    qkv_grad = jnp.concatenate(
        [query_grad, key_grad, value_grad.reshape(length, width_k)], axis=1
    ).astype(jnp.bfloat16)
    grad_qkv = jnp.dot(normed.T, qkv_grad, preferred_element_type=jnp.float32)
    norm_one_grad = jnp.dot(qkv_grad, qkv_back.T, preferred_element_type=jnp.float32)
    grad_gain_one = jnp.sum(norm_one_grad * norm_one, axis=0)
    scaled_one = norm_one_grad * gain_af
    input_grad = middle_grad + rstd_one * (
        scaled_one - norm_one * jnp.mean(scaled_one * norm_one, axis=-1, keepdims=True)
    )
    grad_tokens = input_grad.astype(jnp.bfloat16)
    owned = (
        lax.psum_scatter(
            grad_gain_one.astype(jnp.bfloat16), "shard", scatter_dimension=0, tiled=True
        ).astype(jnp.float32),
        lax.psum_scatter(
            grad_gain_two.astype(jnp.bfloat16), "shard", scatter_dimension=0, tiled=True
        ).astype(jnp.float32),
        lax.psum_scatter(
            grad_qkv.astype(jnp.bfloat16), "shard", scatter_dimension=0, tiled=True
        ).astype(jnp.float32),
        lax.psum_scatter(
            grad_out.astype(jnp.bfloat16), "shard", scatter_dimension=1, tiled=True
        ).astype(jnp.float32),
        lax.psum_scatter(
            grad_router.astype(jnp.bfloat16), "shard", scatter_dimension=0, tiled=True
        ).astype(jnp.float32),
        lax.psum_scatter(
            grad_gate_up.astype(jnp.bfloat16), "shard", scatter_dimension=1, tiled=True
        ).astype(jnp.float32),
        lax.psum_scatter(
            grad_down.astype(jnp.bfloat16), "shard", scatter_dimension=2, tiled=True
        ).astype(jnp.float32),
    )
    summed = tuple(
        (
            lax.psum(owned[0].astype(jnp.bfloat16), "replica").astype(jnp.float32),
            lax.psum(owned[1].astype(jnp.bfloat16), "replica").astype(jnp.float32),
            lax.psum(owned[2].astype(jnp.bfloat16), "replica").astype(jnp.float32),
            lax.psum(owned[3].astype(jnp.bfloat16), "replica").astype(jnp.float32),
            lax.psum(owned[4].astype(jnp.bfloat16), "replica").astype(jnp.float32),
            lax.psum(owned[5].astype(jnp.bfloat16), "replica").astype(jnp.float32),
            lax.psum(owned[6].astype(jnp.bfloat16), "replica").astype(jnp.float32),
        )
    )
    return (
        layer_out,
        grad_tokens,
        summed[0],
        summed[1],
        summed[2],
        summed[3],
        summed[4],
        summed[5],
        summed[6],
    )


def solution(mesh):
    placed = (
        P(("shard", "replica"), None),
        P(("shard", "replica"), None),
        P("shard"),
        P("shard"),
        P("shard", None),
        P(None, "shard"),
        P("shard", None),
        P(None, "shard", None),
        P(None, None, "shard"),
        P(("shard", "replica"), None),
        P(("shard", "replica"), None),
    )
    return jax.shard_map(
        shards,
        mesh=mesh,
        in_specs=placed,
        out_specs=(
            P(("shard", "replica"), None),
            P(("shard", "replica"), None),
            P("shard"),
            P("shard"),
            P("shard", None),
            P(None, "shard"),
            P("shard", None),
            P(None, "shard", None),
            P(None, None, "shard"),
        ),
        check_vma=False,
    )
```

profile of v0, /device:TPU:8, one launch (start us, length us, event | category | flops | bytes accessed | tf_op | source)
XLA Modules:
  0.0 1337.5 jit_solution(17703155118275848143)
XLA Ops:
  10.1 14.9 %all-gather = bf16[8,1,128]{2,1,0:T(2,128)(2,1)S(1)} all-gather(bf16[1,1,128]{2,1,0:T(2,128)(2,1)S(1)} %bitcast.249), channel_id=1, replica_groups=mesh['shard'=8,'replica'=32] {'shard'}, dimensions={0}, use_global_device_ids=true | all-gather | bytes 2304 | tf_op jit(solution)/shard_map/all_gather | solution.py:75
  26.1 10.6 all-gather.1
  37.0 7.1 gather_fusion
  47.6 5.2 scatter_custom_fusion
  53.2 5.2 scatter_custom_fusion.1
  58.5 5.6 gather_fusion.4
  64.2 13.3 all_gather.25
  88.8 17.8 %all-gather.9.cloned.1.call-done = bf16[1024,1024]{1,0:T(8,128)(2,1)} async-done(((bf16[1024,128]{1,0:T(8,128)(2,1)}), bf16[1024,1024]{1,0:T(8,128)(2,1)}) %all-gather.9.cloned.1.call-update) | async-done | bytes 2097168 | tf_op jit(solution)/shard_map/all_gather | solution.py:78
  109.1 6.2 gather_fusion.1
  115.5 10.2 gather_fusion.6
  125.9 172.1 %all-gather.11.cloned.1.call-done = bf16[10,1024,1024]{2,1,0:T(8,128)(2,1)} async-done(((bf16[10,128,1024]{2,1,0:T(8,128)(2,1)}), bf16[10,1024,1024]{2,1,0:T(8,128)(2,1)}) %all-gather.11.cloned.1.call-update) | async-done | bytes 20971536 | tf_op jit(solution)/shard_map/all_gather | solution.py:80
  298.0 9.6 fusion.96
  311.2 97.5 %all-gather.13.cloned.1.call-done = bf16[10,512,1024]{2,1,0:T(8,128)(2,1)} async-done(((bf16[10,512,128]{2,1,0:T(8,128)(2,1)}), bf16[10,512,1024]{2,1,0:T(8,128)(2,1)}) %all-gather.13.cloned.1.call-update) | async-done | bytes 10485776 | tf_op jit(solution)/shard_map/all_gather | solution.py:81
  408.7 5.7 fusion.97
  417.5 9.4 gather_fusion.2
  436.0 8.2 gather_fusion.3
  444.4 13.1 multiply_convert_fusion.3
  457.5 13.7 %fusion.39 = f32[10,144,1024]{2,1,0:T(8,128)} fusion(bf16[10,1024,1024]{2,1,0:T(8,128)(2,1)} %all-gather.11.cloned.1.call-done, bf16[10,144,512]{2,1,0:T(8,128)(2,1)} %get-tuple-element.167, bf16[10,144,512]{2,1,0:T(8,128)(2,1)} %get-tuple-element.166), kind=kOutput, calls=%fused_computation.70 | convolution fusion | flops 3025797120 | bytes 29818880 | tf_op jit(solution)/shard_map/ecf,edf->ecd/dot_general | solution.py:162
  471.3 6.2 concatenate.53
  477.5 9.4 gather_fusion.5
  498.5 8.6 convolution_convert_fusion.1
  507.2 22.6 %copy.174 = bf16[10,512,1024]{1,0,2:T(8,128)(2,1)} copy(bf16[10,512,1024]{2,1,0:T(8,128)(2,1)} %convolution_convert_fusion.1) | data formatting | bytes 20971520
  529.8 19.6 %copy.178 = bf16[128,8,10,512]{3,1,2,0:T(8,128)(2,1)} copy(bf16[128,8,10,512]{3,2,1,0:T(8,128)(2,1)} %bitcast.211) | data formatting | bytes 20971520
  559.1 43.9 %while.15 = (s32[]{:T(128)}, f32[8,160,2,64]{1,3,2,0:T(8,128)}, f32[8,160,64]{1,2,0:T(8,128)}, bf16[8,160,64]{1,2,0:T(8,128)(2,1)}, bf16[8,160,64]{1,2,0:T(8,128...) while((s32[]{:T(128)}, f32[8,160,2,64]{1,3,2,0:T(8,128)}, ...), condition=%wide.region_18.19_spmd.clone, body=%wide.region_16.18_spmd.clone.sunk | while | flops 33284800 | bytes 2544753 | solution.py:224
  613.9 12.4 convolution_convert_fusion
  630.2 34.1 %reduce-scatter.20.cloned.1.call-done = bf16[128,5120]{1,0:T(8,128)(2,1)} async-done(((bf16[1024,5120]{1,0:T(8,128)(2,1)}), bf16[128,5120]{1,0:T(8,128)(2,1)}) %reduce-scatter.20.cloned.1.call-update) | async-done | bytes 1310736
  669.6 54.5 %reduce-scatter.12.cloned.1.call-done = bf16[128,2048]{1,0:T(8,128)(2,1)} async-done(((bf16[1024,2048]{1,0:T(8,128)(2,1)}), bf16[128,2048]{1,0:T(8,128)(2,1)}) %reduce-scatter.12.cloned.1.call-update) | async-done | bytes 524304 | tf_op jit(solution)/shard_map/reduce_scatter | solution.py:248
  724.1 227.0 %reduce-scatter.14.cloned.1.call-done = bf16[10,128,1024]{2,1,0:T(8,128)(2,1)} async-done(((bf16[10,1024,1024]{2,1,0:T(8,128)(2,1)}), bf16[10,128,1024]{2,1,0:T(8,128)(2,1)}) %reduce-scatter.14.cloned.1.call-update) | async-done | bytes 2621456 | tf_op jit(solution)/shard_map/reduce_scatter | solution.py:257
  956.3 14.3 %all-reduce.8 = (bf16[1024]{0:T(1024)(128)(2,1)S(1)}, bf16[1024]{0:T(1024)(128)(2,1)S(1)}) all-reduce(bf16[1024]{0:T(1024)(128)(2,1)S(1)} %get-tuple-element.133, bf16[1024]{0:T(1024)(128)(2,1)S(1)} %get-tuple-element.131), channel_id=2, replica_groups=mesh['shard'=8,'replica'=32] {'shard'}, use_global_device_ids=true, to_apply=%region_21.22.clone | all-reduce | flops 2048 | bytes 8192
  971.7 17.4 %reduce-scatter.18.cloned.1.call-done = bf16[128,10]{1,0:T(8,128)(2,1)} async-done(((bf16[1024,10]{1,0:T(8,128)(2,1)}), bf16[128,10]{1,0:T(8,128)(2,1)}) %reduce-scatter.18.cloned.1.call-update) | async-done | bytes 2576
  990.0 78.5 %all-reduce.6 = (bf16[128]{0:T(256)(128)(2,1)S(1)}, bf16[128]{0:T(256)(128)(2,1)S(1)}, bf16[128,10]{0,1:T(8,128)(2,1)S(1)}) all-reduce(bf16[128]{0:T(256)(128)(2,1)S(1)} %dynamic-slice.1, bf16[128]{0:T(256)(128)(2,1)S(1)} %dynamic-slice.3, bf16[128,10]{0,1:T(8,128)(2,1)S(1)} %copy.173), channel_id=1, replica_groups=mesh['shard'=8,'replica'=32] {'replica'}, use_global_device_ids=true, to_apply=%region_22.23 | all-reduce | flops 1536 | bytes 6144 | tf_op jit(solution)/shard_map/psum | solution.py:266
  1070.2 249.6 %all-reduce.11.cloned.1.call-done = (bf16[128,2048]{1,0:T(8,128)(2,1)}, bf16[1024,128]{1,0:T(8,128)(2,1)}, bf16[10,128,1024]{2,1,0:T(8,128)(2,1)}, bf16[10,512,128]{2,1,0:T(8,128)(2,1)}) async-done(((bf16[128,2048]{1,0:T(8,128)(2,1)}, bf16[1024,128]{1,0:T(8,128)(2,1)}, bf16[10,128,1024]{2,1,0:T(8,128)(2,1)}, bf16[10,512,128]{2,1,0:T(8,128)(2,1)}), (bf16[128,2048]{1,0:T(8,128)(2,1)}, ...) | async-done | bytes 4718608 | tf_op jit(solution)/shard_map/psum | solution.py:268
  (285 shorter events, 140.9 us)
Async XLA Ops:
  7.2 18.9 %copy-start.42 = (bf16[128]{0:T(256)(128)(2,1)S(1)}, bf16[128]{0:T(256)(128)(2,1)}, u32[]{:S(2)}) copy-start(bf16[128]{0:T(256)(128)(2,1)} %param.16) | copy-start | bytes 772
  7.2 29.5 %copy-start.29 = (s32[160,8]{0,1:T(8,128)S(1)}, s32[160,8]{0,1:T(8,128)}, u32[]{:S(2)}) copy-start(s32[160,8]{0,1:T(8,128)} %param.22) | copy-start | bytes 15364
  7.2 29.7 %copy-start.39 = (s32[1,1280]{1,0:T(1,128)S(1)}, s32[1,1280]{1,0:T(1,128)}, u32[]{:S(2)}) copy-start(s32[1,1280]{1,0:T(1,128)} %param.23) | copy-start | bytes 15364
  7.2 70.5 %all-gather.7.cloned.1.call-start = ((), (), s32[]{:S(2)}) async-start(), calls=%async_computation.5 | async-start | bytes 4718592 | tf_op jit(solution)/shard_map/all_gather | solution.py:77
  8.0 98.7 %all-gather.9.cloned.1.call-start = ((), (), s32[]{:S(2)}) async-start(), calls=%async_computation.6 | async-start | bytes 2359296 | tf_op jit(solution)/shard_map/all_gather | solution.py:78
  8.7 289.3 %all-gather.11.cloned.1.call-start = ((), (), s32[]{:S(2)}) async-start(), calls=%async_computation.7 | async-start | bytes 23592960 | tf_op jit(solution)/shard_map/all_gather | solution.py:80
  9.4 399.2 %all-gather.13.cloned.1.call-start = ((), (), s32[]{:S(2)}) async-start(), calls=%async_computation.8 | async-start | bytes 11796480 | tf_op jit(solution)/shard_map/all_gather | solution.py:81
  10.0 618.4 %reduce-scatter.16.cloned.1.call-start = ((), (), s32[]{:S(2)}) async-start(), calls=%async_computation.11 | async-start | bytes 2359296
  25.0 52.7 %copy-start.32 = (f32[8,1,128]{2,1,0:T(1,128)}, f32[8,1,128]{2,1,0:T(1,128)S(1)}, u32[]{:S(2)}) copy-start(f32[8,1,128]{2,1,0:T(1,128)S(1)} %convert_element_type.241) | copy-start | bytes 12292
  25.8 60.7 %copy-start.26 = (f32[160,32]{0,1:T(8,128)}, f32[160,32]{0,1:T(8,128)S(1)}, u32[]{:S(2)}) copy-start(f32[160,32]{0,1:T(8,128)S(1)} %get-tuple-element.182) | copy-start | bytes 61444
  26.0 56.4 %copy-start.21 = (f32[160,32]{1,0:T(8,128)}, f32[160,32]{1,0:T(8,128)S(1)}, u32[]{:S(2)}) copy-start(f32[160,32]{1,0:T(8,128)S(1)} %copy.142) | copy-start | bytes 61444
  37.0 16.1 %copy-start.6 = (bf16[160,1024]{1,0:T(8,128)(2,1)S(1)}, bf16[160,1024]{1,0:T(8,128)(2,1)}, u32[]{:S(2)}) copy-start(bf16[160,1024]{1,0:T(8,128)(2,1)} %param.14) | copy-start | bytes 983044
  58.5 5.7 copy-start.40
  58.5 19.0 %copy-start.2 = (bf16[160,1024]{1,0:T(8,128)(2,1)S(1)}, bf16[160,1024]{1,0:T(8,128)(2,1)}, u32[]{:S(2)}) copy-start(bf16[160,1024]{1,0:T(8,128)(2,1)} %param.13) | copy-start | bytes 983044
  88.8 20.1 %copy-start.12 = (bf16[8,64,2,160]{3,1,2,0:T(8,128)(2,1)}, bf16[8,64,2,160]{3,1,2,0:T(8,128)(2,1)S(1)}, u32[]{:S(2)}) copy-start(bf16[8,64,2,160]{3,1,2,0:T(8,128)(2,1)S(1)} %fusion.41) | copy-start | bytes 983044
  109.0 6.2 copy-start.8
  486.9 4.5 copy-start.11
  492.5 63.9 %copy-start.3 = (f32[160,1024]{1,0:T(8,128)}, f32[160,1024]{1,0:T(8,128)S(1)}, u32[]{:S(2)}) copy-start(f32[160,1024]{1,0:T(8,128)S(1)} %get-tuple-element.172) | copy-start | bytes 1966084
  498.5 165.8 %reduce-scatter.20.cloned.1.call-start = ((), (), s32[]{:S(2)}) async-start(), calls=%async_computation.13 | async-start | bytes 11796480
  549.3 6.3 copy-start.35
  549.4 7.0 copy-start.5
  549.4 174.7 %reduce-scatter.12.cloned.1.call-start = ((), (), s32[]{:S(2)}) async-start(), calls=%async_computation.9 | async-start | bytes 4718592 | tf_op jit(solution)/shard_map/reduce_scatter | solution.py:248
  559.1 45.1 %copy-start.27 = (f32[160,32]{0,1:T(8,128)S(1)}, f32[160,32]{0,1:T(8,128)}, u32[]{:S(2)}) copy-start(f32[160,32]{0,1:T(8,128)} %copy-done.26) | copy-start | bytes 61444
  559.1 45.1 %copy-start.31 = (f32[160,32]{0,1:T(8,128)S(1)}, f32[160,32]{0,1:T(8,128)}, u32[]{:S(2)}) copy-start(f32[160,32]{0,1:T(8,128)} %get-tuple-element.180) | copy-start | bytes 61444
  612.0 339.0 %reduce-scatter.14.cloned.1.call-start = ((), (), s32[]{:S(2)}) async-start(), calls=%async_computation.10 | async-start | bytes 23592960 | tf_op jit(solution)/shard_map/reduce_scatter | solution.py:257
  626.3 362.9 %reduce-scatter.18.cloned.1.call-start = ((), (), s32[]{:S(2)}) async-start(), calls=%async_computation.12 | async-start | bytes 294912
  628.3 691.4 %all-reduce.11.cloned.1.call-start = ((), (), s32[]{:S(2)}) async-start(), calls=%async_computation.14 | async-start | bytes 9437184 | tf_op jit(solution)/shard_map/psum | solution.py:268
  669.6 281.5 %copy-start.43 = (u32[256]{0:T(256)S(1)}, u32[256]{0:T(256)}, u32[]{:S(2)}) copy-start(u32[256]{0:T(256)} %constant.141) | copy-start | bytes 3076
  669.6 282.8 %copy-start.15 = (bf16[160,1024]{1,0:T(8,128)(2,1)S(1)}, bf16[160,1024]{1,0:T(8,128)(2,1)}, u32[]{:S(2)}) copy-start(bf16[160,1024]{1,0:T(8,128)(2,1)} %copy-done.14) | copy-start | bytes 983044
  669.6 282.8 %copy-start.24 = (bf16[160,512]{1,0:T(8,128)(2,1)S(1)}, bf16[160,512]{1,0:T(8,128)(2,1)}, u32[]{:S(2)}) copy-start(bf16[160,512]{1,0:T(8,128)(2,1)} %copy-done.23) | copy-start | bytes 491524
  952.4 18.4 %copy-start.4 = (f32[160,1024]{1,0:T(8,128)S(1)}, f32[160,1024]{1,0:T(8,128)}, u32[]{:S(2)}) copy-start(f32[160,1024]{1,0:T(8,128)} %copy-done.3) | copy-start | bytes 1966084
  1323.6 4.9 copy-start.17
  (23 other events, 48.1 us)
Sparse Core Ops, SparseCore 0:
  9.9 55.9 all-gather.6
  67.7 38.8 all-gather.8
  108.5 189.5 all-gather.10
  299.7 108.8 all-gather.12
  498.6 43.0 reduce-scatter.15
  549.5 114.7 reduce-scatter.19
  667.4 56.6 reduce-scatter.11
  726.7 224.3 reduce-scatter.13
  954.2 34.9 reduce-scatter.17
  993.3 326.3 all-reduce.10
where the time goes:
time: 1350 us; the launch traced here: 1340 us
  waiting for transfers between devices  873 us (65%)
  local copies, waits for them, and re-layouts  151 us (11%)
  blocking collectives  132 us (10%)
  matrix products  129 us (10%)
  other arithmetic  36.8 us (3%)
  between operations  16.2 us (1%)
    psum x1, waiting for transfers between devices, shards(): lax.psum(owned[2].astype(jnp.bfloat16), 'replica').astype(jnp.float32)  250 us
    reduce_scatter x1, waiting for transfers between devices, shards(): lax.psum_scatter(grad_gate_up.astype(jnp.bfloat16), 'shard', scatter_dime...  227 us
    all_gather x1, waiting for transfers between devices, shards(): lax.all_gather(shard_parts[5], 'shard', axis=1, tiled=True)  172 us
    all_gather x1, waiting for transfers between devices, shards(): lax.all_gather(shard_parts[6], 'shard', axis=2, tiled=True)  97.5 us
    psum x1, blocking collectives, shards(): lax.psum(owned[0].astype(jnp.bfloat16), 'replica').astype(jnp.float32)  78.5 us
    unnamed x103, local copies, waits for them, and re-layouts  65.4 us
    reduce_scatter x1, waiting for transfers between devices, shards(): lax.psum_scatter(grad_qkv.astype(jnp.bfloat16), 'shard', scatter_dimensio...  54.5 us
    unnamed x13, waiting for transfers between devices  54.3 us
  transfers between devices with their start and end apart: 10, of which 8 were waited for; matrix products, arithmetic and copies ran while one was open for 16% of the time, Pallas kernels for 0%

commit v1 on v0

v1 whole, which is shorter than its diff:
```python
import math

import jax
import jax.numpy as jnp
from jax import lax
from jax.sharding import Mesh
from jax.sharding import PartitionSpec as P

D = 1024
HEADS = 16
KV_HEADS = 8
HD = 64
F = 512
TOPK = 8
EXPERTS = 10
CAP = 144
TOK = 160
EPSILON = 1e-06
ROPE_BASE = 10000.0

AXES = ("zh", "core", "x", "zl", "y")
SIZES = (4, 2, 4, 2, 4)
BF = jnp.bfloat16
F32 = jnp.float32


def dot(a, b, ca=1, cb=0):
    return lax.dot_general(a, b, (((ca,), (cb,)), ((), ())), preferred_element_type=F32)


def take(v, axis, k):
    return lax.ppermute(v, axis, [((i + k) % 4, i) for i in range(4)])


def ring_gather(v, axis):
    return [v] + [take(v, axis, k) for k in (1, 2, 3)]


def ring_return(blocks, axis):
    return [blocks[0]] + [take(blocks[(4 - k) % 4], axis, k) for k in (1, 2, 3)]


def keep_plan(routes, order):
    pairs = TOK * TOPK
    expert_row = routes.reshape(1, pairs)
    place = (lax.broadcasted_iota(jnp.int32, (pairs, pairs), 0) == order).astype(BF)
    named = (lax.broadcasted_iota(jnp.int32, (16, pairs), 0) == expert_row).astype(BF)
    ordered = dot(named, place)
    before = (
        lax.broadcasted_iota(jnp.int32, (pairs, pairs), 0)
        < lax.broadcasted_iota(jnp.int32, (pairs, pairs), 1)
    ).astype(BF)
    earlier = dot(ordered.astype(BF), before)
    kept = jnp.where(earlier < CAP, ordered, 0.0).astype(BF)
    kept_pair = dot(kept, place, 1, 1).astype(BF)
    owner = (
        lax.broadcasted_iota(jnp.int32, (TOK, pairs), 1) // TOPK
        == lax.broadcasted_iota(jnp.int32, (TOK, pairs), 0)
    ).astype(BF)
    kept_token = dot(owner, kept_pair, 1, 1)
    lane = lax.broadcasted_iota(jnp.int32, (TOK, 16), 1)
    routed = jnp.zeros((TOK, 16), F32)
    for r in range(TOPK):
        routed = routed + (routes[:, r : r + 1] == lane).astype(F32)
    return routed, kept_token


def rope_tables():
    half = HD // 2
    position = jnp.arange(TOK).astype(F32)[:, None]
    frequency = ROPE_BASE ** (-jnp.arange(half).astype(F32) / half)
    angles = position * frequency[None, :]
    return jnp.cos(angles), jnp.sin(angles)


def rotate(values, cosine, sine, direction):
    rows, width = values.shape
    v = values.reshape(rows // TOK, TOK, width // HD, 2, HD // 2)
    a, b = v[:, :, :, 0], v[:, :, :, 1]
    c = cosine[None, :, None, :]
    s = direction * sine[None, :, None, :]
    return jnp.stack([a * c - b * s, b * c + a * s], axis=3).reshape(rows, width)


def rms(v):
    return lax.rsqrt(jnp.mean(v * v, axis=-1, keepdims=True) + EPSILON)


def attention_units():
    for seq in range(4):
        for kv in range(2):
            yield seq, kv


def softmax_of(q, k):
    scores = dot(q, k, 1, 1) * (1.0 / math.sqrt(HD))
    rows = lax.broadcasted_iota(jnp.int32, (TOK, TOK), 0)
    cols = lax.broadcasted_iota(jnp.int32, (TOK, TOK), 1)
    scores = jnp.where(rows >= cols, scores, -1e30)
    peak = jnp.max(scores, axis=-1, keepdims=True)
    e = jnp.exp(scores - peak)
    return e / jnp.sum(e, axis=-1, keepdims=True)


def attention_forward(tok_all, gain, w, cosine, sine):
    x = tok_all.astype(F32)
    h1 = (x * rms(x) * gain).astype(BF)
    qkv = dot(h1, w)
    qk = rotate(qkv[:, :384], cosine, sine, 1.0).astype(BF)
    vv = qkv[:, 384:].astype(BF)
    out = []
    for seq in range(4):
        rows = slice(seq * TOK, seq * TOK + TOK)
        cols = []
        for head in range(4):
            kv = head // 2
            q = qk[rows, head * HD : head * HD + HD]
            k = qk[rows, 256 + kv * HD : 256 + kv * HD + HD]
            v = vv[rows, kv * HD : kv * HD + HD]
            cols.append(dot(softmax_of(q, k).astype(BF), v))
        out.append(jnp.concatenate(cols, axis=1))
    return h1, qk, vv, jnp.concatenate(out, axis=0).astype(BF)


def attention_backward(qk, vv, d_att, cosine, sine):
    scale = 1.0 / math.sqrt(HD)
    dq_all, dk_all, dv_all = [], [], []
    for seq in range(4):
        rows = slice(seq * TOK, seq * TOK + TOK)
        dqs, dks, dvs = [], [0.0, 0.0], [0.0, 0.0]
        for head in range(4):
            kv = head // 2
            q = qk[rows, head * HD : head * HD + HD]
            k = qk[rows, 256 + kv * HD : 256 + kv * HD + HD]
            v = vv[rows, kv * HD : kv * HD + HD]
            da = d_att[rows, head * HD : head * HD + HD]
            p = softmax_of(q, k)
            dp = dot(da, v, 1, 1)
            dvs[kv] = dvs[kv] + dot(p.astype(BF), da, 0, 0)
            ds = (p * (dp - jnp.sum(p * dp, axis=-1, keepdims=True))).astype(BF)
            dqs.append(dot(ds, k) * scale)
            dks[kv] = dks[kv] + dot(ds, q, 0, 0) * scale
        dq_all.append(jnp.concatenate(dqs, axis=1))
        dk_all.append(jnp.concatenate(dks, axis=1))
        dv_all.append(jnp.concatenate(dvs, axis=1))
    dqk = jnp.concatenate([jnp.concatenate(dq_all, 0), jnp.concatenate(dk_all, 0)], axis=1)
    dqk = rotate(dqk, cosine, sine, -1.0)
    return jnp.concatenate([dqk, jnp.concatenate(dv_all, 0)], axis=1).astype(BF)


def post_attention(tok, att, w_out, gain, w_router_t, routed, kept):
    middle = tok.astype(F32)
    for k in range(4):
        middle = middle + dot(att[k], w_out[k])
    rstd = rms(middle)
    h2 = (middle * rstd * gain).astype(BF)
    logits = dot(h2, w_router_t, 1, 1)
    masked = jnp.where(routed > 0.5, logits, -1e30)
    e = jnp.where(routed > 0.5, jnp.exp(masked - jnp.max(masked, axis=-1, keepdims=True)), 0.0)
    gates = e / jnp.sum(e, axis=-1, keepdims=True)
    weight = gates * kept
    high = weight.astype(BF)
    low = (weight - high.astype(F32)).astype(BF)
    pad = jnp.zeros((TOK, 128 - 2 * 16), BF)
    return middle, rstd, gates, jnp.concatenate([h2, high, low, pad], axis=1)


def moe_inner(h2_all, weight, c_all, w_gu, w_dn):
    gu = dot(h2_all, w_gu).reshape(-1, EXPERTS, 2, 128)
    g, u = gu[:, :, 0], gu[:, :, 1]
    s = 1.0 / (1.0 + jnp.exp(-g))
    act = (g * s * u).astype(BF)
    cw = dot(c_all, w_dn, 1, 1).reshape(-1, EXPERTS, 128)
    d_gates = jnp.sum(act.astype(F32) * cw, axis=2)
    wt = weight[:, :EXPERTS, None]
    d_act = cw * wt
    d_g = d_act * u * s * (1.0 + g * (1.0 - s))
    d_u = d_act * (g * s)
    d_gu = jnp.stack([d_g, d_u], axis=2).astype(BF).reshape(-1, EXPERTS * 256)
    wact = (act.astype(F32) * wt).astype(BF).reshape(-1, EXPERTS * 128)
    d_h2 = dot(d_gu, w_gu, 1, 1)
    return d_h2, d_gates, d_gu, wact


def local(tokens, cotangent, gain_one, gain_two, w_qkv, w_out, w_router, w_gate_up, w_down, routes, slot_order):
    xi = lax.axis_index("x")
    yi = lax.axis_index("y")
    ci = lax.axis_index("core")
    tok_all = jnp.concatenate(ring_gather(tokens, "x"), axis=0)
    heads = w_qkv[:, : 1024].reshape(128, 4, 2, 128)
    q_tiles = lax.dynamic_index_in_dim(heads, xi, 1, False)
    kv_tiles = lax.dynamic_index_in_dim(w_qkv[:, 1024:].reshape(128, 2, 4, 128), xi, 2, False)
    tiles = jnp.concatenate([q_tiles, kv_tiles], axis=1)
    qkv_tile = lax.dynamic_index_in_dim(tiles, yi, 1, False)
    out_rows = lax.dynamic_slice(w_out, (xi * 256 + yi * 64, 0), (64, 128))
    misc = jnp.concatenate([gain_one[None], gain_two[None], w_router.T, jnp.zeros((4, 128), BF)], axis=0)
    small = jnp.concatenate([qkv_tile, out_rows, misc], axis=0)
    small_all = lax.all_gather(small, ("zh", "core", "y"), axis=0).reshape(4, 2, 4, 208, 128)
    w_att = small_all[:, :, :, :128].transpose(0, 1, 3, 2, 4).reshape(1024, 512)
    w_o0 = small_all[:, :, :, 128:192].transpose(2, 3, 0, 1, 4).reshape(256, 1024)
    misc_all = small_all[:, :, 0, 192:].transpose(2, 0, 1, 3).reshape(16, 1024)
    w_o = ring_gather(w_o0, "x")
    gain_a = misc_all[0:1].astype(F32)
    gain_b = misc_all[1:2].astype(F32)
    router_t = jnp.concatenate([misc_all[2:12], jnp.zeros((6, D), BF)], axis=0)
    gu_local = w_gate_up.reshape(10, 128, 2, 4, 128)
    gu_x = lax.dynamic_index_in_dim(gu_local, xi, 3, False).transpose(0, 2, 1, 3).reshape(4, 5 * 128, 128)
    gu_xy = lax.dynamic_index_in_dim(gu_x, yi, 0, False)
    dn_x = lax.dynamic_index_in_dim(w_down.reshape(10, 4, 4, 32, 128), xi, 1, False)
    dn_xy = lax.dynamic_index_in_dim(dn_x, yi, 1, False).reshape(320, 128)
    experts = jnp.concatenate([gu_xy, dn_xy], axis=0)
    experts_z = lax.all_gather(experts, "zh", axis=0)
    experts_all = lax.all_gather(experts_z, ("core", "y"), axis=0).reshape(2, 4, 4, 960, 128)
    w_gu = experts_all[:, :, :, :640].reshape(2, 4, 4, 5, 128, 128).transpose(2, 0, 4, 1, 3, 5).reshape(1024, 2560)
    w_dn = experts_all[:, :, :, 640:].reshape(2, 4, 4, 10, 32, 128).transpose(3, 1, 4, 2, 0, 5).reshape(1280, 1024)

    routed, kept = keep_plan(routes, slot_order)
    cosine, sine = rope_tables()
    h1_all, qk, vv, att_all = attention_forward(tok_all, gain_a, w_att, cosine, sine)
    att = ring_return(list(att_all.reshape(4, TOK, 256)), "x")
    middle, rstd_two, gates, h2_ext = post_attention(tokens, att, w_o, gain_b, router_t, routed, kept)
    ext_all = jnp.concatenate(ring_gather(h2_ext, "x"), axis=0)
    c_all = jnp.concatenate(ring_gather(cotangent, "x"), axis=0)
    h2_all = ext_all[:, :1024]
    weight = ext_all[:, 1024:1040].astype(F32) + ext_all[:, 1040:1056].astype(F32)
    d_h2_part, d_gates_part, d_gu, wact = moe_inner(h2_all, weight, c_all, w_gu, w_dn)
    high = d_gates_part.astype(BF)
    low = (d_gates_part - high.astype(F32)).astype(BF)
    zero6 = jnp.zeros((4 * TOK, 6), BF)
    payload = jnp.concatenate([d_h2_part.astype(BF), high, zero6, low, zero6, jnp.zeros((4 * TOK, 96), BF)], axis=1)
    back = ring_return(list(payload.reshape(4, TOK, 1152)), "x")
    back = sum(b.astype(F32) for b in back)
    mix_part = dot(wact, w_dn).astype(BF)
    mix = ring_return(list(mix_part.reshape(4, TOK, 1024)), "x")
    layer_out = (middle + sum(m.astype(F32) for m in mix)).astype(BF)
    g_gu = dot(h2_all, d_gu, 0, 0).astype(BF)
    g_dn = dot(wact, c_all, 0, 0).astype(BF)
    upstream = cotangent.astype(F32)
    h2 = h2_ext[:, :1024]
    d_gates = (back[:, 1024:1040] + back[:, 1040:1056]) * kept
    d_logits = (gates * (d_gates - jnp.sum(gates * d_gates, axis=1, keepdims=True))).astype(BF)
    g_router = dot(d_logits, h2, 0, 0)
    d_h2 = back[:, :1024] + dot(d_logits, router_t)
    norm_two = middle * rstd_two
    g_gain_two = jnp.sum(d_h2 * norm_two, axis=0, keepdims=True)
    u2 = d_h2 * gain_b
    d_middle = upstream + rstd_two * (u2 - norm_two * jnp.mean(u2 * norm_two, axis=-1, keepdims=True))
    d_mid_all = jnp.concatenate(ring_gather(d_middle.astype(BF), "x"), axis=0)
    d_att = dot(d_mid_all, w_o0, 1, 1).astype(BF)
    d_qkv = attention_backward(qk, vv, d_att, cosine, sine)
    g_qkv = dot(h1_all, d_qkv, 0, 0)
    g_out = dot(att_all, d_mid_all, 0, 0)
    d_h1_part = dot(d_qkv, w_att, 1, 1)
    tf = tok_all.astype(F32)
    g_gain_one = jnp.sum(d_h1_part * (tf * rms(tf)), axis=0, keepdims=True)
    d_h1 = ring_return(list(d_h1_part.astype(BF).reshape(4, TOK, 1024)), "x")
    d_h1 = sum(b.astype(F32) for b in d_h1)
    x = tokens.astype(F32)
    rstd_one = rms(x)
    norm_one = x * rstd_one
    u1 = d_h1 * gain_a
    grad_tokens = (d_middle + rstd_one * (u1 - norm_one * jnp.mean(u1 * norm_one, axis=-1, keepdims=True))).astype(BF)

    def fold(v, n):
        other = lax.ppermute(lax.dynamic_index_in_dim(v, 1 - ci, 0, False), "core", [(0, 1), (1, 0)])
        mine = lax.dynamic_index_in_dim(v, ci, 0, False)
        return (mine.astype(F32) + other.astype(F32)).astype(BF)

    def fold_z(v, n):
        v = jnp.broadcast_to(v[:, None], (4, 2, n, 128)).reshape(8, n, 128)
        v = lax.all_to_all(v, ("zh", "zl"), 0, 0, tiled=True)
        return jnp.sum(v.astype(F32), axis=0).astype(BF)

    e_gu = g_gu.reshape(4, 2, 128, 4, 5, 128).transpose(1, 3, 0, 4, 2, 5).reshape(2, 4, 4, 640, 128)
    e_dn = g_dn.reshape(10, 4, 32, 4, 2, 128).transpose(4, 1, 3, 0, 2, 5).reshape(2, 4, 4, 320, 128)
    e = fold(jnp.concatenate([e_gu, e_dn], axis=3), 960)
    e = lax.psum_scatter(e, "y", scatter_dimension=0, tiled=False)
    e = fold_z(e, 960)
    e = lax.all_gather(e, ("x", "y"), axis=0).reshape(4, 4, 960, 128)
    grad_gate_up = (
        e[:, :, :640].reshape(4, 10, 2, 128, 128).transpose(1, 3, 2, 0, 4).reshape(10, 128, 1024).astype(F32)
    )
    grad_down = e[:, :, 640:].reshape(4, 4, 10, 32, 128).transpose(2, 0, 1, 3, 4).reshape(10, 512, 128).astype(F32)

    a_qkv = g_qkv.astype(BF).reshape(4, 2, 128, 4, 128).transpose(1, 3, 0, 2, 4)
    a_out = g_out.astype(BF).reshape(4, 64, 4, 2, 128).transpose(3, 0, 2, 1, 4)
    g_misc = jnp.concatenate([g_gain_one, g_gain_two, g_router[:10], jnp.zeros((4, D), F32)], axis=0).astype(BF)
    a_misc = g_misc.reshape(16, 4, 2, 128).transpose(2, 1, 0, 3)[:, None]
    a_misc = jnp.concatenate([a_misc, jnp.zeros((2, 3, 4, 16, 128), BF)], axis=1)
    a = fold(jnp.concatenate([a_qkv, a_out, a_misc], axis=3), 208)
    a = lax.all_to_all(a, "y", 0, 0, tiled=True)
    a = jnp.sum(a.astype(F32), axis=0).astype(BF)
    a = fold_z(a, 208)
    a = lax.all_gather(a, ("x", "y"), axis=0).reshape(4, 4, 208, 128)
    q = a[:, :2, :128].transpose(2, 0, 1, 3).reshape(128, 1024)
    k = a[:, 2, :128].transpose(1, 0, 2).reshape(128, 512)
    v = a[:, 3, :128].transpose(1, 0, 2).reshape(128, 512)
    grad_qkv = jnp.concatenate([q, k, v], axis=1).astype(F32)
    grad_out = a[:, :, 128:192].reshape(1024, 128).astype(F32)
    m = jnp.sum(a[:, 0, 192:].astype(F32), axis=0)
    return (layer_out, grad_tokens, m[0], m[1], grad_qkv, grad_out, m[2:12].T, grad_gate_up, grad_down)


def solution(mesh):
    fine = Mesh(mesh.devices.reshape(SIZES), AXES)
    rows = P(AXES, None)
    shard = ("zh", "core")
    return jax.shard_map(
        local,
        mesh=fine,
        in_specs=(
            rows, rows, P(shard), P(shard), P(shard, None), P(None, shard), P(shard, None),
            P(None, shard, None), P(None, None, shard), rows, rows,
        ),
        out_specs=(
            rows, rows, P(shard), P(shard), P(shard, None), P(None, shard), P(shard, None),
            P(None, shard, None), P(None, None, shard),
        ),
        check_vma=False,
    )
```

time: 1350 us -> 651 us (0.48)
  waiting for transfers between devices: 873 us -> 107 us
  blocking collectives: 132 us -> 48.9 us
  starting transfers between devices: 0.4 us -> 74.6 us
  local copies, waits for them, and re-layouts: 151 us -> 200 us
  other arithmetic: 36.8 us -> 63.7 us
    all_gather x4 -> x3, waiting for transfers between devices: 287 us -> 7.35 us  [the longest x1 7.35 us: local(): lax.all_gather(small, ('zh', 'core', 'y'), axis=0)]
    reduce_scatter x2 -> x1, waiting for transfers between devices: 281 us -> 24.8 us  [local(): e = lax.psum_scatter(e, 'y', scatter_dimension=0, tiled=False)]
    psum x1 -> x0, waiting for transfers between devices: 250 us -> none  [shards(): lax.psum(owned[2].astype(jnp.bfloat16), 'replica').astype(jnp.float32)]
    psum x1 -> x0, blocking collectives: 78.5 us -> none  [shards(): lax.psum(owned[0].astype(jnp.bfloat16), 'replica').astype(jnp.float32)]
    gather x11 -> x0, local copies, waits for them, and re-layouts: 56.6 us -> none  [the longest x5 10.6 us: shards(): chosen = jnp.take_along_axis(logits, routes, axis=1)]
    ppermute x0 -> x29, starting transfers between devices: none -> 54.3 us  [the longest x27 54 us: take(): return lax.ppermute(v, axis, [((i + k) % 4, i) for i in range(4)])]
    unnamed x13 -> x4, waiting for transfers between devices: 54.3 us -> 0.07 us
    ppermute x0 -> x29, waiting for transfers between devices: none -> 47.8 us  [the longest x27 47.8 us: take(): return lax.ppermute(v, axis, [((i + k) % 4, i) for i in range(4)])]
  transfers between devices with their start and end apart: 10 -> 36, of which waited for: 8 -> 14; matrix products, arithmetic and copies ran while one was open for 16% -> 39% of each run, Pallas kernels for 0% -> 0%
where the time goes in v1:
time: 651 us; the launch traced here: 640 us
  local copies, waits for them, and re-layouts  200 us (31%)
  matrix products  128 us (20%)
  waiting for transfers between devices  107 us (16%)
  starting transfers between devices  74.6 us (11%)
  other arithmetic  63.7 us (10%)
  blocking collectives  48.9 us (8%)
  between operations  17.7 us (3%)
    dot_general x117, matrix products, dot(): lax.dot_general(a, b, (((ca,), (cb,)), ((), ())), preferred_element_type=...  128 us
    ppermute x27, starting transfers between devices, take(): return lax.ppermute(v, axis, [((i + k) % 4, i) for i in range(4)])  54 us
    ppermute x27, waiting for transfers between devices, take(): return lax.ppermute(v, axis, [((i + k) % 4, i) for i in range(4)])  47.8 us
    unnamed x516, local copies, waits for them, and re-layouts  29.7 us
    all_gather x1, blocking collectives, local(): experts_z = lax.all_gather(experts, 'zh', axis=0)  25.7 us
    reduce_scatter x1, waiting for transfers between devices, local(): e = lax.psum_scatter(e, 'y', scatter_dimension=0, tiled=False)  24.8 us
    all_to_all x2, waiting for transfers between devices, fold_z(): v = lax.all_to_all(v, ('zh', 'zl'), 0, 0, tiled=True)  23.8 us
    all_gather x1, blocking collectives, local(): a = lax.all_gather(a, ('x', 'y'), axis=0).reshape(4, 4, 208, 128)  23.2 us
  transfers between devices with their start and end apart: 36, of which 14 were waited for; matrix products, arithmetic and copies ran while one was open for 39% of the time, Pallas kernels for 0%

profile of v1, /device:TPU:8, one launch (start us, length us, event | category | flops | bytes accessed | tf_op | source)
XLA Modules:
  0.0 639.6 jit_solution(8982483642601723436)
XLA Ops:
  28.1 25.7 %all-gather.1 = bf16[3840,128]{1,0:T(8,128)(2,1)} all-gather(bf16[960,128]{1,0:T(8,128)(2,1)S(1)} %pad_maximum_fusion.6), channel_id=3, replica_groups=mesh['zh'=4,'core'=2,'x'=4,'zl'=2,'y'=4] {'zh'}, dimensions={0}, use_global_device_ids=true | all-gather | bytes 1228800 | tf_op jit(solution)/shard_map/all_gather | solution.py:212
  64.6 7.3 %all-gather.9.cloned.1.call-done = bf16[6656,128]{1,0:T(8,128)(2,1)} async-done(((bf16[208,128]{1,0:T(8,128)(2,1)}), bf16[6656,128]{1,0:T(8,128)(2,1)}) %all-gather.9.cloned.1.call-update) | async-done | bytes 1703952 | tf_op jit(solution)/shard_map/all_gather | solution.py:198
  116.6 4.7 collective-permute-done.7
  121.3 15.3 %collective-permute-start.3 = (bf16[160,256]{0,1:T(8,128)(2,1)S(1)}, bf16[160,256]{0,1:T(8,128)(2,1)S(1)}, u32[]{:S(2)}, u32[]{:S(2)}) collective-permute-start(bf16[160,256]{0,1:T(8,128)(2,1)S(1)} %pad_maximum_fusion.7), channel_id=1, source_target_pairs={{8,0},{16,8},{24,16},{0,24},{9,1},{17,9},{25,17},{1,25},{10,2},{18... | collective-permute-start | bytes 245768 | tf_op jit(solution)/shard_map/ppermute | solution.py:32
  142.6 5.1 collective-permute-start.10
  165.4 6.4 %pad_maximum_fusion = bf16[640,1152]{0,1:T(8,128)(2,1)} fusion(bf16[160,1152]{0,1:T(8,128)(2,1)S(1)} %copy.214, bf16[160,1152]{0,1:T(8,128)(2,1)} %copy.213, bf16[160,1152]{0,1:T(8,128)(2,1)} %copy.212, bf16[160,96]{0,1:T(8,128)(2,1)S(1)} %broadcast_in_dim.75, bf16[160,16]{0,1:T(8,128)(2,1)S(1)} %get-tuple-element.86, ...), kind=kLoop, calls=%fused_computation.71 | loop fusion | flops 10321920 | bytes 2949120 | tf_op jit(solution)/shard_map/concatenate | solution.py:222
  175.3 5.4 slice.503
  180.7 13.6 %copy.217 = bf16[4,2,128,4,5,128]{2,1,0,5,4,3:T(2,128)(2,1)} copy(bf16[4,2,128,4,5,128]{5,2,4,0,3,1:T(8,128)(2,1)} %bitcast.291) | data formatting | bytes 10485760 | tf_op jit(solution)/shard_map/transpose | solution.py:214
  194.3 9.3 %reshape.433 = bf16[1024,2560]{0,1:T(8,128)(2,1)} reshape(bf16[4,2,128,4,5,128]{2,1,0,5,4,3:T(2,128)(2,1)} %copy.217) | data formatting | bytes 10485760 | tf_op jit(solution)/shard_map/reshape | solution.py:214
  203.7 5.9 copy.220
  209.6 5.4 dot_general.422
  215.0 6.8 %fusion.42 = f32[640,10,2,128]{0,3,2,1:T(8,128)S(1)} fusion(bf16[10,2,128,1024]{3,2,1,0:T(8,128)(2,1)} %bitcast.299, bf16[640,1152]{0,1:T(8,128)(2,1)} %pad_maximum_fusion), kind=kOutput, calls=%fused_computation.79 | convolution fusion | flops 3355443200 | bytes 13107200 | tf_op jit(solution)/shard_map/dot_general | solution.py:28
  231.0 5.6 convolution_convert_fusion.2
  241.4 5.4 reshape.447
  250.6 10.9 %concatenate.142 = bf16[640,1152]{0,1:T(8,128)(2,1)} concatenate(bf16[640,1024]{0,1:T(8,128)(2,1)} %convolution_convert_fusion.2, bf16[640,10]{0,1:T(8,128)(2,1)S(1)} %get-tuple-element.57, bf16[640,6]{0,1:T(8,128)(2,1)S(1)} %broadcast_in_dim.76, bf16[640,10]{0,1:T(8,128)(2,1)S(1)} %get-tuple-element.56, bf16[640,6]{0,1:T(8,128)(2,1)S(1)} %broadcast_in_dim.76, ...), dimensions={1} | concatenate | bytes 2949120 | tf_op jit(solution)/shard_map/concatenate | solution.py:230
  273.5 8.9 %convolution_convert_fusion = bf16[1024,2560]{1,0:T(8,128)(2,1)} fusion(bf16[640,2560]{0,1:T(8,128)(2,1)} %bitcast.309, bf16[640,1152]{0,1:T(8,128)(2,1)} %pad_maximum_fusion), kind=kOutput, calls=%fused_computation.12 | convolution fusion | flops 3358064640 | bytes 9830400 | tf_op jit(solution)/shard_map/dot_general | solution.py:28
  282.4 8.0 %copy.243 = bf16[1024,2560]{0,1:T(8,128)(2,1)} copy(bf16[1024,2560]{1,0:T(8,128)(2,1)} %convolution_convert_fusion) | data formatting | bytes 10485760 | tf_op jit(solution)/shard_map/convert_element_type | solution.py:236
  290.4 9.3 %reshape.445 = bf16[4,2,128,4,5,128]{2,1,0,5,4,3:T(2,128)(2,1)} reshape(bf16[1024,2560]{0,1:T(8,128)(2,1)} %copy.243) | data formatting | bytes 10485760 | tf_op jit(solution)/shard_map/reshape | solution.py:274
  299.7 13.7 %copy.244 = bf16[2,4,4,5,128,128]{5,4,3,2,1,0:T(8,128)(2,1)} copy(bf16[2,4,4,5,128,128]{4,0,2,5,3,1:T(2,128)(2,1)} %bitcast.292) | data formatting | bytes 10485760 | tf_op jit(solution)/shard_map/transpose | solution.py:274
  330.9 13.7 %collective-permute-done.23 = bf16[160,1024]{0,1:T(8,128)(2,1)} collective-permute-done((bf16[160,1024]{0,1:T(8,128)(2,1)}, bf16[160,1024]{0,1:T(8,128)(2,1)}, u32[]{:S(2)}, u32[]{:S(2)}) %collective-permute-start.23) | collective-permute-done | bytes 327712 | tf_op jit(solution)/shard_map/ppermute | solution.py:32
  395.0 24.8 %reduce-scatter.2.cloned.1.call-done = bf16[1,4,960,128]{3,2,1,0:T(8,128)(2,1)} async-done(((bf16[4,4,960,128]{3,2,1,0:T(8,128)(2,1)}), bf16[1,4,960,128]{3,2,1,0:T(8,128)(2,1)}) %reduce-scatter.2.cloned.1.call-update) | async-done | bytes 983056 | tf_op jit(solution)/shard_map/reduce_scatter | solution.py:277
  422.5 7.1 %all-to-all-start.2 = ((bf16[8,960,128]{2,1,0:T(8,128)(2,1)}), bf16[8,960,128]{2,1,0:T(8,128)(2,1)}, u32[]{:S(2)}, u32[]{:S(2)}) async-start(bf16[8,960,128]{2,1,0:T(8,128)(2,1)} %bitcast.298), calls=%async_computation.3 | async-start | bytes 3932160 | tf_op jit(solution)/shard_map/all_to_all | solution.py:271
  430.4 4.8 maximum_maximum_fusion
  454.5 23.8 %all-to-all-done.2 = bf16[8,960,128]{2,1,0:T(8,128)(2,1)} async-done(((bf16[8,960,128]{2,1,0:T(8,128)(2,1)}), bf16[8,960,128]{2,1,0:T(8,128)(2,1)}, u32[]{:S(2)}, u32[]{:S(2)}) %all-to-all-start.2) | async-done | bytes 1966112 | tf_op jit(solution)/shard_map/all_to_all | solution.py:271
  504.6 5.4 reshape.435
  523.8 5.9 all-to-all-start
  544.3 6.6 %all-to-all-start.1 = ((bf16[8,208,128]{2,1,0:T(8,128)(2,1)}), bf16[8,208,128]{2,1,0:T(8,128)(2,1)}, u32[]{:S(2)}, u32[]{:S(2)}) async-start(bf16[8,208,128]{2,1,0:T(8,128)(2,1)} %bitcast.317), calls=%async_computation.1 | async-start | bytes 851968 | tf_op jit(solution)/shard_map/all_to_all | solution.py:271
  556.6 7.8 %collective-permute-done.12 = bf16[160,1024]{0,1:T(8,128)(2,1)} collective-permute-done((bf16[160,1024]{0,1:T(8,128)(2,1)}, bf16[160,1024]{0,1:T(8,128)(2,1)}, u32[]{:S(2)}, u32[]{:S(2)}) %collective-permute-start.12) | collective-permute-done | bytes 327712 | tf_op jit(solution)/shard_map/ppermute | solution.py:32
  565.5 11.5 %collective-permute-done.13 = bf16[160,1024]{0,1:T(8,128)(2,1)S(1)} collective-permute-done((bf16[160,1024]{0,1:T(8,128)(2,1)}, bf16[160,1024]{0,1:T(8,128)(2,1)S(1)}, u32[]{:S(2)}, u32[]{:S(2)}) %collective-permute-start.13) | collective-permute-done | bytes 327712 | tf_op jit(solution)/shard_map/ppermute | solution.py:32
  585.4 23.2 %all-gather.3 = bf16[3328,128]{1,0:T(8,128)(2,1)S(1)} all-gather(bf16[208,128]{1,0:T(8,128)(2,1)S(1)} %reduce_sum.534), channel_id=5, replica_groups=mesh['zh'=4,'core'=2,'x'=4,'zl'=2,'y'=4] {'x','y'}, dimensions={0}, use_global_device_ids=true | all-gather | bytes 905216 | tf_op jit(solution)/shard_map/all_gather | solution.py:294
  620.9 6.0 copy.246
  626.8 6.0 copy.250
  (853 shorter events, 302.5 us)
Async XLA Ops:
  7.2 64.7 %all-gather.9.cloned.1.call-start = ((), (), s32[]{:S(2)}) async-start(), calls=%async_computation.5 | async-start | bytes 1757184 | tf_op jit(solution)/shard_map/all_gather | solution.py:198
  14.3 157.6 %all-gather.11.cloned.1.call-start = ((), (), s32[]{:S(2)}) async-start(), calls=%async_computation.6 | async-start | bytes 8847360 | tf_op jit(solution)/shard_map/all_gather | solution.py:213
  14.3 135.1 %collective-permute-start.16 = (bf16[160,1024]{1,0:T(8,128)(2,1)}, bf16[160,1024]{1,0:T(8,128)(2,1)}, u32[]{:S(2)}, u32[]{:S(2)}) collective-permute-start(bf16[160,1024]{1,0:T(8,128)(2,1)} %param.12), channel_id=1, source_target_pairs={{16,0},{24,8},{0,16},{8,24},{17,1},{25,9},{1,17},{9,25},{18,2},{26... | collective-permute-start | bytes 983048 | tf_op jit(solution)/shard_map/ppermute | solution.py:32
  17.4 130.3 %collective-permute-start.15 = (bf16[160,1024]{1,0:T(8,128)(2,1)}, bf16[160,1024]{1,0:T(8,128)(2,1)}, u32[]{:S(2)}, u32[]{:S(2)}) collective-permute-start(bf16[160,1024]{1,0:T(8,128)(2,1)} %param.12), channel_id=1, source_target_pairs={{8,0},{16,8},{24,16},{0,24},{9,1},{17,9},{25,17},{1,25},{10,2},{18... | collective-permute-start | bytes 983048 | tf_op jit(solution)/shard_map/ppermute | solution.py:32
  18.6 44.5 %collective-permute-start.1 = (bf16[160,1024]{1,0:T(8,128)(2,1)S(1)}, bf16[160,1024]{1,0:T(8,128)(2,1)}, u32[]{:S(2)}, u32[]{:S(2)}) collective-permute-start(bf16[160,1024]{1,0:T(8,128)(2,1)S(1)} %copy-done.16), channel_id=1, source_target_pairs={{16,0},{24,8},{0,16},{8,24},{17,1},{25,9},{1,17},{9,25},{18,2},{26... | collective-permute-start | bytes 983048 | tf_op jit(solution)/shard_map/ppermute | solution.py:32
  20.1 43.0 %collective-permute-start = (bf16[160,1024]{1,0:T(8,128)(2,1)S(1)}, bf16[160,1024]{1,0:T(8,128)(2,1)}, u32[]{:S(2)}, u32[]{:S(2)}) collective-permute-start(bf16[160,1024]{1,0:T(8,128)(2,1)S(1)} %copy-done.16), channel_id=1, source_target_pairs={{8,0},{16,8},{24,16},{0,24},{9,1},{17,9},{25,17},{1,25},{10,2},{18... | collective-permute-start | bytes 983048 | tf_op jit(solution)/shard_map/ppermute | solution.py:32
  22.1 40.9 %collective-permute-start.2 = (bf16[160,1024]{1,0:T(8,128)(2,1)S(1)}, bf16[160,1024]{1,0:T(8,128)(2,1)}, u32[]{:S(2)}, u32[]{:S(2)}) collective-permute-start(bf16[160,1024]{1,0:T(8,128)(2,1)S(1)} %copy-done.16), channel_id=1, source_target_pairs={{24,0},{0,8},{8,16},{16,24},{25,1},{1,9},{9,17},{17,25},{26,2},{2,... | collective-permute-start | bytes 983048 | tf_op jit(solution)/shard_map/ppermute | solution.py:32
  53.8 365.9 %reduce-scatter.2.cloned.1.call-start = ((), (), s32[]{:S(2)}) async-start(), calls=%async_computation.4 | async-start | bytes 4915200 | tf_op jit(solution)/shard_map/reduce_scatter | solution.py:277
  78.7 42.6 %collective-permute-start.8 = (bf16[256,1024]{1,0:T(8,128)(2,1)}, bf16[256,1024]{1,0:T(8,128)(2,1)}, u32[]{:S(2)}, u32[]{:S(2)}) collective-permute-start(bf16[256,1024]{1,0:T(8,128)(2,1)} %reshape.426), channel_id=1, source_target_pairs={{24,0},{0,8},{8,16},{16,24},{25,1},{1,9},{9,17},{17,25},{26,2},{2,... | collective-permute-start | bytes 1572872 | tf_op jit(solution)/shard_map/ppermute | solution.py:32
  84.1 31.1 %collective-permute-start.6 = (bf16[256,1024]{1,0:T(8,128)(2,1)}, bf16[256,1024]{1,0:T(8,128)(2,1)}, u32[]{:S(2)}, u32[]{:S(2)}) collective-permute-start(bf16[256,1024]{1,0:T(8,128)(2,1)} %reshape.426), channel_id=1, source_target_pairs={{16,0},{24,8},{0,16},{8,24},{17,1},{25,9},{1,17},{9,25},{18,2},{26... | collective-permute-start | bytes 1572872 | tf_op jit(solution)/shard_map/ppermute | solution.py:32
  93.5 19.6 %collective-permute-start.5 = (bf16[160,256]{0,1:T(8,128)(2,1)S(1)}, bf16[160,256]{0,1:T(8,128)(2,1)S(1)}, u32[]{:S(2)}, u32[]{:S(2)}) collective-permute-start(bf16[160,256]{0,1:T(8,128)(2,1)S(1)} %pad_maximum_fusion.8), channel_id=1, source_target_pairs={{16,0},{24,8},{0,16},{8,24},{17,1},{25,9},{1,17},{9,25},{18,2},{26... | collective-permute-start | bytes 245768 | tf_op jit(solution)/shard_map/ppermute | solution.py:32
  113.1 26.0 %collective-permute-start.4 = (bf16[256,1024]{1,0:T(8,128)(2,1)}, bf16[256,1024]{1,0:T(8,128)(2,1)S(1)}, u32[]{:S(2)}, u32[]{:S(2)}) collective-permute-start(bf16[256,1024]{1,0:T(8,128)(2,1)} %reshape.426), channel_id=1, source_target_pairs={{8,0},{16,8},{24,16},{0,24},{9,1},{17,9},{25,17},{1,25},{10,2},{18... | collective-permute-start | bytes 1572872 | tf_op jit(solution)/shard_map/ppermute | solution.py:32
  121.3 29.9 %collective-permute-start.17 = (bf16[160,1024]{1,0:T(8,128)(2,1)}, bf16[160,1024]{1,0:T(8,128)(2,1)}, u32[]{:S(2)}, u32[]{:S(2)}) collective-permute-start(bf16[160,1024]{1,0:T(8,128)(2,1)} %param.12), channel_id=1, source_target_pairs={{24,0},{0,8},{8,16},{16,24},{25,1},{1,9},{9,17},{17,25},{26,2},{2,... | collective-permute-start | bytes 983048 | tf_op jit(solution)/shard_map/ppermute | solution.py:32
  121.3 17.8 %collective-permute-start.3 = (bf16[160,256]{0,1:T(8,128)(2,1)S(1)}, bf16[160,256]{0,1:T(8,128)(2,1)S(1)}, u32[]{:S(2)}, u32[]{:S(2)}) collective-permute-start(bf16[160,256]{0,1:T(8,128)(2,1)S(1)} %pad_maximum_fusion.7), channel_id=1, source_target_pairs={{8,0},{16,8},{24,16},{0,24},{9,1},{17,9},{25,17},{1,25},{10,2},{18... | collective-permute-start | bytes 245768 | tf_op jit(solution)/shard_map/ppermute | solution.py:32
  142.6 17.9 %collective-permute-start.10 = (bf16[160,1152]{1,0:T(8,128)(2,1)S(1)}, bf16[160,1152]{1,0:T(8,128)(2,1)}, u32[]{:S(2)}, u32[]{:S(2)}) collective-permute-start(bf16[160,1152]{1,0:T(8,128)(2,1)S(1)} %copy.209), channel_id=1, source_target_pairs={{16,0},{24,8},{0,16},{8,24},{17,1},{25,9},{1,17},{9,25},{18,2},{26... | collective-permute-start | bytes 1105928 | tf_op jit(solution)/shard_map/ppermute | solution.py:32
  269.5 43.9 %collective-permute-start.19 = (bf16[160,1152]{1,0:T(8,128)(2,1)}, bf16[160,1152]{1,0:T(8,128)(2,1)S(1)}, u32[]{:S(2)}, u32[]{:S(2)}) collective-permute-start(bf16[160,1152]{1,0:T(8,128)(2,1)} %copy.228), channel_id=1, source_target_pairs={{16,0},{24,8},{0,16},{8,24},{17,1},{25,9},{1,17},{9,25},{18,2},{26... | collective-permute-start | bytes 1105928 | tf_op jit(solution)/shard_map/ppermute | solution.py:32
  270.1 44.5 %collective-permute-start.20 = (bf16[160,1152]{1,0:T(8,128)(2,1)S(1)}, bf16[160,1152]{1,0:T(8,128)(2,1)}, u32[]{:S(2)}, u32[]{:S(2)}) collective-permute-start(bf16[160,1152]{1,0:T(8,128)(2,1)S(1)} %copy.230), channel_id=1, source_target_pairs={{24,0},{0,8},{8,16},{16,24},{25,1},{1,9},{9,17},{17,25},{26,2},{2,... | collective-permute-start | bytes 1105928 | tf_op jit(solution)/shard_map/ppermute | solution.py:32
  270.6 46.1 %collective-permute-start.18 = (bf16[160,1152]{1,0:T(8,128)(2,1)}, bf16[160,1152]{1,0:T(8,128)(2,1)}, u32[]{:S(2)}, u32[]{:S(2)}) collective-permute-start(bf16[160,1152]{1,0:T(8,128)(2,1)} %copy.226), channel_id=1, source_target_pairs={{8,0},{16,8},{24,16},{0,24},{9,1},{17,9},{25,17},{1,25},{10,2},{18... | collective-permute-start | bytes 1105928 | tf_op jit(solution)/shard_map/ppermute | solution.py:32
  322.6 22.0 %collective-permute-start.23 = (bf16[160,1024]{0,1:T(8,128)(2,1)}, bf16[160,1024]{0,1:T(8,128)(2,1)}, u32[]{:S(2)}, u32[]{:S(2)}) collective-permute-start(bf16[160,1024]{0,1:T(8,128)(2,1)} %fusion.411), channel_id=1, source_target_pairs={{24,0},{0,8},{8,16},{16,24},{25,1},{1,9},{9,17},{17,25},{26,2},{2,... | collective-permute-start | bytes 983048 | tf_op jit(solution)/shard_map/ppermute | solution.py:32
  322.6 22.0 %collective-permute-start.22 = (bf16[160,1024]{0,1:T(8,128)(2,1)}, bf16[160,1024]{0,1:T(8,128)(2,1)}, u32[]{:S(2)}, u32[]{:S(2)}) collective-permute-start(bf16[160,1024]{0,1:T(8,128)(2,1)} %fusion.411), channel_id=1, source_target_pairs={{16,0},{24,8},{0,16},{8,24},{17,1},{25,9},{1,17},{9,25},{18,2},{26... | collective-permute-start | bytes 983048 | tf_op jit(solution)/shard_map/ppermute | solution.py:32
  324.4 20.8 %collective-permute-start.21 = (bf16[160,1024]{0,1:T(8,128)(2,1)}, bf16[160,1024]{0,1:T(8,128)(2,1)}, u32[]{:S(2)}, u32[]{:S(2)}) collective-permute-start(bf16[160,1024]{0,1:T(8,128)(2,1)} %fusion.411), channel_id=1, source_target_pairs={{8,0},{16,8},{24,16},{0,24},{9,1},{17,9},{25,17},{1,25},{10,2},{18... | collective-permute-start | bytes 983048 | tf_op jit(solution)/shard_map/ppermute | solution.py:32
  329.2 41.4 %collective-permute-start.28 = (bf16[4,4,960,128]{3,2,1,0:T(8,128)(2,1)}, bf16[4,4,960,128]{3,2,1,0:T(8,128)(2,1)}, u32[]{:S(2)}, u32[]{:S(2)}) collective-permute-start(bf16[4,4,960,128]{3,2,1,0:T(8,128)(2,1)} %fusion.5), channel_id=1, source_target_pairs={{0,32},{32,0},{1,33},{33,1},{2,34},{34,2},{3,35},{35,3},{4,36},{36... | collective-permute-start | bytes 11796488 | tf_op jit(solution)/shard_map/ppermute | solution.py:265
  422.5 55.7 %all-to-all-start.2 = ((bf16[8,960,128]{2,1,0:T(8,128)(2,1)}), bf16[8,960,128]{2,1,0:T(8,128)(2,1)}, u32[]{:S(2)}, u32[]{:S(2)}) async-start(bf16[8,960,128]{2,1,0:T(8,128)(2,1)} %bitcast.298), calls=%async_computation.3 | async-start | bytes 3932160 | tf_op jit(solution)/shard_map/all_to_all | solution.py:271
  429.7 182.6 %all-gather.13.cloned.1.call-start = ((), (), s32[]{:S(2)}) async-start(), calls=%async_computation.7 | async-start | bytes 4177920 | tf_op jit(solution)/shard_map/all_gather | solution.py:279
  516.5 34.4 %collective-permute-start.24 = (bf16[160,1024]{0,1:T(8,128)(2,1)}, bf16[160,1024]{0,1:T(8,128)(2,1)}, u32[]{:S(2)}, u32[]{:S(2)}) collective-permute-start(bf16[160,1024]{0,1:T(8,128)(2,1)} %get-tuple-element.71), channel_id=1, source_target_pairs={{8,0},{16,8},{24,16},{0,24},{9,1},{17,9},{25,17},{1,25},{10,2},{18... | collective-permute-start | bytes 983048 | tf_op jit(solution)/shard_map/ppermute | solution.py:32
  519.1 34.6 %collective-permute-start.26 = (bf16[160,1024]{0,1:T(8,128)(2,1)}, bf16[160,1024]{0,1:T(8,128)(2,1)}, u32[]{:S(2)}, u32[]{:S(2)}) collective-permute-start(bf16[160,1024]{0,1:T(8,128)(2,1)} %get-tuple-element.72), channel_id=1, source_target_pairs={{24,0},{0,8},{8,16},{16,24},{25,1},{1,9},{9,17},{17,25},{26,2},{2,... | collective-permute-start | bytes 983048 | tf_op jit(solution)/shard_map/ppermute | solution.py:32
  519.1 35.7 %collective-permute-start.25 = (bf16[160,1024]{0,1:T(8,128)(2,1)}, bf16[160,1024]{0,1:T(8,128)(2,1)}, u32[]{:S(2)}, u32[]{:S(2)}) collective-permute-start(bf16[160,1024]{0,1:T(8,128)(2,1)} %get-tuple-element.73), channel_id=1, source_target_pairs={{16,0},{24,8},{0,16},{8,24},{17,1},{25,9},{1,17},{9,25},{18,2},{26... | collective-permute-start | bytes 983048 | tf_op jit(solution)/shard_map/ppermute | solution.py:32
  523.8 18.3 %all-to-all-start = ((bf16[4,4,208,128]{3,2,1,0:T(8,128)(2,1)}), bf16[4,4,208,128]{3,2,1,0:T(8,128)(2,1)}, u32[]{:S(2)}, u32[]{:S(2)}) async-start(bf16[4,4,208,128]{3,2,1,0:T(8,128)(2,1)} %fusion.37), calls=%async_computation | async-start | bytes 1703936 | tf_op jit(solution)/shard_map/all_to_all | solution.py:291
  537.2 27.3 %collective-permute-start.12 = (bf16[160,1024]{0,1:T(8,128)(2,1)}, bf16[160,1024]{0,1:T(8,128)(2,1)}, u32[]{:S(2)}, u32[]{:S(2)}) collective-permute-start(bf16[160,1024]{0,1:T(8,128)(2,1)} %get-tuple-element.74), channel_id=1, source_target_pairs={{8,0},{16,8},{24,16},{0,24},{9,1},{17,9},{25,17},{1,25},{10,2},{18... | collective-permute-start | bytes 983048 | tf_op jit(solution)/shard_map/ppermute | solution.py:32
  538.3 27.1 %collective-permute-start.14 = (bf16[160,1024]{0,1:T(8,128)(2,1)}, bf16[160,1024]{0,1:T(8,128)(2,1)}, u32[]{:S(2)}, u32[]{:S(2)}) collective-permute-start(bf16[160,1024]{0,1:T(8,128)(2,1)} %get-tuple-element.75), channel_id=1, source_target_pairs={{24,0},{0,8},{8,16},{16,24},{25,1},{1,9},{9,17},{17,25},{26,2},{2,... | collective-permute-start | bytes 983048 | tf_op jit(solution)/shard_map/ppermute | solution.py:32
  544.3 40.1 %all-to-all-start.1 = ((bf16[8,208,128]{2,1,0:T(8,128)(2,1)}), bf16[8,208,128]{2,1,0:T(8,128)(2,1)}, u32[]{:S(2)}, u32[]{:S(2)}) async-start(bf16[8,208,128]{2,1,0:T(8,128)(2,1)} %bitcast.317), calls=%async_computation.1 | async-start | bytes 851968 | tf_op jit(solution)/shard_map/all_to_all | solution.py:271
  550.9 26.0 %collective-permute-start.13 = (bf16[160,1024]{0,1:T(8,128)(2,1)}, bf16[160,1024]{0,1:T(8,128)(2,1)S(1)}, u32[]{:S(2)}, u32[]{:S(2)}) collective-permute-start(bf16[160,1024]{0,1:T(8,128)(2,1)} %get-tuple-element.76), channel_id=1, source_target_pairs={{16,0},{24,8},{0,16},{8,24},{17,1},{25,9},{1,17},{9,25},{18,2},{26... | collective-permute-start | bytes 983048 | tf_op jit(solution)/shard_map/ppermute | solution.py:32
  (254 other events, 2533.7 us)
Sparse Core Ops, SparseCore 0:
  14.4 57.5 all-gather.8
  73.8 47.5 all-gather.10
  374.8 44.8 reduce-scatter.1
  481.0 60.6 all-gather.12
